TPU v7x, 1024 devices: a whole 4x8x16 slice. The times are simulated.
1024 devices in a mesh: row: 32 (over x, z_hi, core), col: 32 (over z_lo, y).
Axes of the slice: x: 4, y: 8, z: 16 (z_hi: 4, z_lo: 4; z = z_hi * 4 + z_lo), core: 2. Of those that a mesh axis runs over, the one named last changes fastest.
Arguments:
- inputs: bfloat16 [512, 12288], P(None, 'row'), may hold values from -6 to 6
- cotangent: bfloat16 [512, 12288], P(None, 'row'), may hold values from -6 to 6
- w_in: bfloat16 [12288, 24576], P('row', 'col'), may hold values from -0.0546875 to 0.0546875
- w_out: bfloat16 [24576, 12288], P('col', 'row'), may hold values from -0.0390625 to 0.0390625
Outputs:
- mlp_out: float32 [512, 12288], P('col', 'row')
- input_grad: float32 [512, 12288], P('col', 'row')
- w_in_grad: float32 [12288, 24576], P('row', 'col')
- w_out_grad: float32 [24576, 12288], P('col', 'row')
All inputs are finite; a program needn't handle non-finite values.
Results may differ from a plain program's by a relative error of at most 0.0029.
Values may be sent and summed in bfloat16 or wider, within the bound.
No kernel may reach another device: no remote copies, remote signals or barrier semaphores. Data moves between devices by JAX's collectives and lax.ppermute only.
A program may use at most 32 MiB of HBM per device.

v0:
```python
import jax
import jax.numpy as jnp
from jax import lax
from jax.sharding import PartitionSpec as P

inv_root_two = 0.7071067811865476
density_scale = 0.3989422804014327


def gelu_value(pre):
    return pre * 0.5 * (1.0 + lax.erf(pre * inv_root_two))


def gelu_slope(pre):
    return 0.5 * (1.0 + lax.erf(pre * inv_root_two)) + pre * density_scale * jnp.exp(
        -0.5 * pre * pre
    )


def row_section(partial_fn, total_rows, finish):
    summed = lax.psum(partial_fn(0, total_rows), "row")
    return (finish(summed), summed)


def col_section(partial_fn, total_rows):
    return lax.psum_scatter(
        partial_fn(jnp.int32(0), total_rows // lax.axis_size("col") * lax.axis_size("col")),
        "col",
        scatter_dimension=0,
        tiled=True,
    )


def contract_last(left, right):
    return lax.dot_general(
        left, right, (((1,), (1,)), ((), ())), preferred_element_type=jnp.float32
    )


def contract_first(left, right):
    return lax.dot_general(
        left, right, (((0,), (0,)), ((), ())), preferred_element_type=jnp.float32
    )


def shards(inputs, cotangent, w_in, w_out):
    total_rows = inputs.shape[0]

    def pre_term(first_row, row_count):
        return jnp.dot(inputs, w_in, preferred_element_type=jnp.float32)

    def finish_forward(value):
        return gelu_value(value).astype(jnp.bfloat16)

    act_all, pre_local = row_section(pre_term, total_rows, finish_forward)

    def grad_term(first_row, row_count):
        return contract_last(cotangent, w_out)

    def finish_backward(value):
        return (value * gelu_slope(pre_local)).astype(jnp.bfloat16)

    pre_grad_all, ignored = row_section(grad_term, total_rows, finish_backward)

    def out_term(first_row, row_count):
        return jnp.dot(act_all, w_out, preferred_element_type=jnp.float32)

    def back_term(first_row, row_count):
        return contract_last(pre_grad_all, w_in)

    mlp_out = col_section(out_term, total_rows)
    w_out_grad = contract_first(act_all, cotangent)
    w_in_grad = contract_first(inputs, pre_grad_all)
    input_grad = col_section(back_term, total_rows)
    return (mlp_out, input_grad, w_in_grad, w_out_grad)


def solution(mesh):
    in_specs = (P(None, "row"), P(None, "row"), P("row", "col"), P("col", "row"))
    out_specs = (P("col", "row"), P("col", "row"), P("row", "col"), P("col", "row"))
    return jax.shard_map(shards, mesh=mesh, in_specs=in_specs, out_specs=out_specs, check_vma=False)
```

profile of v0, /device:TPU:2, one launch (start us, length us, event | category | flops | bytes accessed | tf_op | source)
XLA Modules:
  0.0 734.3 jit_solution(4336739821371442365)
XLA Ops:
  7.2 0.0 copy-start
  7.2 0.0 copy-start.1
  7.2 0.0 copy-start.2
  7.2 0.0 all-reduce.3.cloned.1.call-start
  7.2 1.0 copy-done
  8.2 2.7 fusion.5
  10.9 0.0 copy-done.1
  11.0 0.0 copy-done.2
  11.0 1.8 fusion.7
  12.7 0.0 all-reduce.3.cloned.1.call-update
  12.7 0.0 reduce-scatter.5.cloned.1.call-start
  12.8 364.4 %all-reduce.3.cloned.1.call-done = (f32[512,768]{1,0:T(8,128)}, f32[512,768]{1,0:T(8,128)}) async-done(((f32[512,768]{1,0:T(8,128)}, f32[512,768]{1,0:T(8,128)}), (f32[512,768]{1,0:T(8,128)}, f32[512,768]{1,0:T(8,128)})) %all-reduce.3.cloned.1.call-update) | async-done | bytes 3145744 | tf_op jit(solution)/shard_map/psum | solution.py:21
  377.2 2.6 fusion.4
  379.8 1.5 fusion.8
  381.3 0.0 reduce-scatter.5.cloned.1.call-update
  381.3 0.0 reduce-scatter.3.cloned.1.call-start
  381.4 1.5 fusion.6
  382.9 0.0 reduce-scatter.3.cloned.1.call-update
  382.9 1.6 convolution_bitcast_fusion
  384.5 0.0 copy-start.3
  384.5 1.4 copy.8
  385.9 0.0 copy-done.3
  385.9 1.6 fusion.9
  387.5 175.4 %reduce-scatter.5.cloned.1.call-done = f32[16,384]{1,0:T(8,128)} async-done(((f32[512,384]{1,0:T(8,128)}), f32[16,384]{1,0:T(8,128)}) %reduce-scatter.5.cloned.1.call-update) | async-done | bytes 24592 | tf_op jit(solution)/shard_map/reduce_scatter | solution.py:26
  562.9 164.9 %reduce-scatter.3.cloned.1.call-done = f32[16,384]{1,0:T(8,128)} async-done(((f32[512,384]{1,0:T(8,128)}), f32[16,384]{1,0:T(8,128)}) %reduce-scatter.3.cloned.1.call-update) | async-done | bytes 24592 | tf_op jit(solution)/shard_map/reduce_scatter | solution.py:26
Async XLA Ops:
  7.2 1.1 copy-start
  7.2 3.8 copy-start.1
  7.2 3.8 copy-start.2
  7.2 370.0 %all-reduce.3.cloned.1.call-start = ((), (), s32[]{:S(2)}) async-start(), calls=%async_computation.4 | async-start | bytes 6291456 | tf_op jit(solution)/shard_map/psum | solution.py:21
  12.7 550.2 %reduce-scatter.5.cloned.1.call-start = ((), (), s32[]{:S(2)}) async-start(), calls=%async_computation.3 | async-start | bytes 811008 | tf_op jit(solution)/shard_map/reduce_scatter | solution.py:26
  381.3 346.4 %reduce-scatter.3.cloned.1.call-start = ((), (), s32[]{:S(2)}) async-start(), calls=%async_computation.2 | async-start | bytes 811008 | tf_op jit(solution)/shard_map/reduce_scatter | solution.py:26
  384.5 1.4 copy-start.3
Sparse Core Ops, SparseCore 0:
  12.9 364.2 all-reduce.2
  381.5 181.3 reduce-scatter.4
  566.8 160.8 reduce-scatter.2
where the time goes:
time: 734 us
  waiting for transfers between devices  705 us (96%)
  between operations  13.8 us (2%)
  matrix products  10.6 us (1%)
    psum x1, waiting for transfers between devices, row_section(): summed = lax.psum(partial_fn(0, total_rows), 'row')  364 us
    reduce_scatter x2, waiting for transfers between devices, col_section(): lax.psum_scatter(partial_fn(jnp.int32(0), total_rows // lax.axis_size('co...  340 us
  transfers between devices with their start and end apart: 3, of which 3 were waited for; matrix products, arithmetic and copies ran while one was open for 1% of the time, Pallas kernels for 0%

commit v1 on v0

v1 whole, which is shorter than its diff:
```python
import jax
import jax.numpy as jnp
from jax import lax
from jax.sharding import Mesh, PartitionSpec as P

inv_root_two = 0.7071067811865476
density_scale = 0.3989422804014327

root_scale = 512.0
smallest = 1e-37


def gelu_value(pre):
    return pre * 0.5 * (1.0 + lax.erf(pre * inv_root_two))


def gelu_slope(pre):
    return 0.5 * (1.0 + lax.erf(pre * inv_root_two)) + pre * density_scale * jnp.exp(
        -0.5 * pre * pre
    )


def to_root(value):
    root = value * lax.rsqrt(jnp.maximum(jnp.abs(value), smallest))
    return (root * root_scale).astype(jnp.float16)


def from_root(root):
    root = root.astype(jnp.float32) * (1.0 / root_scale)
    return root * jnp.abs(root)


def contract_last(left, right):
    return lax.dot_general(
        left, right, (((1,), (1,)), ((), ())), preferred_element_type=jnp.float32
    )


def contract_first(left, right):
    return lax.dot_general(
        left, right, (((0,), (0,)), ((), ())), preferred_element_type=jnp.float32
    )


def exchange(value, axis):
    pieces = lax.all_to_all(value, axis, 0, 0, tiled=True)
    return pieces.reshape(lax.axis_size(axis), -1, value.shape[-1])


def swap_core(value):
    return lax.ppermute(value, "core", [(0, 1), (1, 0)])


def shards(inputs, cotangent, w_in, w_out):
    total, features = inputs.shape
    hidden = w_in.shape[1]
    half = total // 2
    core = lax.axis_index("core")
    zl, ny = lax.axis_size("zl"), lax.axis_size("y")

    def reorder(array):
        return array.reshape(zl, ny, -1, features).transpose(1, 0, 2, 3).reshape(total, features)

    inputs, cotangent = reorder(inputs), reorder(cotangent)
    in_mine = lax.dynamic_slice(inputs, (core * half, 0), (half, features))
    in_other = lax.dynamic_slice(inputs, ((1 - core) * half, 0), (half, features))
    ct_mine = lax.dynamic_slice(cotangent, (core * half, 0), (half, features))
    ct_other = lax.dynamic_slice(cotangent, ((1 - core) * half, 0), (half, features))

    pre_sent = swap_core(jnp.dot(in_other, w_in, preferred_element_type=jnp.float32))
    grad_sent = swap_core(contract_last(ct_other, w_out))
    pre = jnp.dot(in_mine, w_in, preferred_element_type=jnp.float32) + pre_sent
    grad = contract_last(ct_mine, w_out) + grad_sent

    both = jnp.concatenate([to_root(pre), to_root(grad)], axis=1)
    both = to_root(jnp.sum(from_root(exchange(both, "x")), axis=0))
    both = jnp.sum(from_root(exchange(both, "zh")), axis=0)
    pre, grad = both[:, :hidden], both[:, hidden:]
    act = gelu_value(pre).astype(jnp.bfloat16)
    pre_grad = (grad * gelu_slope(pre)).astype(jnp.bfloat16)
    mine = jnp.concatenate([act, pre_grad], axis=1)
    mine = lax.all_gather(mine, "zh", axis=0, tiled=True)
    mine = lax.all_gather(mine, "x", axis=0, tiled=True)
    other = swap_core(mine)
    low = jnp.where(core == 0, mine, other)
    high = jnp.where(core == 0, other, mine)
    act = jnp.concatenate([low[:, :hidden], high[:, :hidden]], axis=0)
    pre_grad = jnp.concatenate([low[:, hidden:], high[:, hidden:]], axis=0)

    out = jnp.dot(act, w_out, preferred_element_type=jnp.float32)
    back = contract_last(pre_grad, w_in)
    sums = jnp.concatenate([out.astype(jnp.bfloat16), back.astype(jnp.bfloat16)], axis=1)
    sums = jnp.sum(exchange(sums, "y").astype(jnp.float32), axis=0)
    sums = jnp.sum(exchange(sums, "zl"), axis=0)
    w_out_grad = contract_first(act, cotangent)
    w_in_grad = contract_first(inputs, pre_grad)
    return (sums[:, :features], sums[:, features:], w_in_grad, w_out_grad)


def solution(mesh):
    fine = Mesh(mesh.devices.reshape(4, 4, 2, 4, 8), ("x", "zh", "core", "zl", "y"))
    row, col = ("x", "zh", "core"), ("zl", "y")
    in_specs = (P(None, row), P(None, row), P(row, col), P(col, row))
    out_specs = (P(col, row), P(col, row), P(row, col), P(col, row))
    return jax.shard_map(shards, mesh=fine, in_specs=in_specs, out_specs=out_specs, check_vma=False)
```

time: 734 us -> 145 us (0.20)
  the two profiles are of different devices: /device:TPU:2 before, /device:TPU:1 now
where the time goes in v1:
time: 145 us; the launch traced here: 144 us
  blocking collectives  90.5 us (62%)
  starting transfers between devices  35.2 us (24%)
  matrix products  7.08 us (5%)
  local copies, waits for them, and re-layouts  4.25 us (3%)
  waiting for transfers between devices  4.13 us (3%)
  other arithmetic  1.6 us (1%)
    all_to_all x3, blocking collectives, exchange(): pieces = lax.all_to_all(value, axis, 0, 0, tiled=True)  64.4 us
    ppermute x3, starting transfers between devices, swap_core(): return lax.ppermute(value, 'core', [(0, 1), (1, 0)])  31.8 us
    all_gather x1, blocking collectives, shards(): mine = lax.all_gather(mine, 'zh', axis=0, tiled=True)  15.4 us
    all_gather x1, blocking collectives, shards(): mine = lax.all_gather(mine, 'x', axis=0, tiled=True)  10.7 us
    all_to_all x1, starting transfers between devices, exchange(): pieces = lax.all_to_all(value, axis, 0, 0, tiled=True)  3.36 us
  transfers between devices with their start and end apart: 4, of which 3 were waited for; matrix products, arithmetic and copies ran while one was open for 4% of the time, Pallas kernels for 0%

profile of v1, /device:TPU:1, one launch (start us, length us, event | category | flops | bytes accessed | tf_op | source)
XLA Modules:
  0.0 143.7 jit_solution(11671178479225829557)
XLA Ops:
  0.7 1.1 copy.16
  1.9 0.4 fusion.3
  2.3 16.1 %collective-permute-start.1 = (f32[256,768]{1,0:T(8,128)S(1)}, f32[256,768]{1,0:T(8,128)}, u32[]{:S(2)}, u32[]{:S(2)}) collective-permute-start(f32[256,768]{1,0:T(8,128)S(1)} %fusion.3), channel_id=1, source_target_pairs={{0,32},{32,0},{1,33},{33,1},{2,34},{34,2},{3,35},{35,3},{4,36},{36... | collective-permute-start | bytes 2359304 | tf_op jit(solution)/shard_map/ppermute | solution.py:51
  18.4 0.4 fusion.6
  18.8 1.9 %collective-permute-start = (f32[256,768]{1,0:T(8,128)S(1)}, f32[256,768]{1,0:T(8,128)}, u32[]{:S(2)}, u32[]{:S(2)}) collective-permute-start(f32[256,768]{1,0:T(8,128)S(1)} %fusion.6), channel_id=1, source_target_pairs={{0,32},{32,0},{1,33},{33,1},{2,34},{34,2},{3,35},{35,3},{4,36},{36... | collective-permute-start | bytes 2359304 | tf_op jit(solution)/shard_map/ppermute | solution.py:51
  20.7 1.6 %multiply_convert_fusion = f16[256,768]{1,0:T(8,128)(2,1)S(1)} fusion(f32[256,768]{1,0:T(8,128)} %collective-permute-done.1, bf16[768,384]{1,0:T(8,128)(2,1)S(1)} %copy-done.1, bf16[512,384]{1,0:T(8,128)(2,1)S(1)} %bitcast.26, s32[]{:T(128)S(6)} %select_n.21), kind=kOutput, calls=%fused_computation.12 | convolution fusion | flops 152174592 | bytes 1966084 | tf_op jit(solution)/shard_map/dot_general | solution.py:34
  22.3 0.8 collective-permute-done
  23.1 1.6 %multiply_convert_fusion.1 = f16[256,768]{1,0:T(8,128)(2,1)S(1)} fusion(f32[256,768]{1,0:T(8,128)} %collective-permute-done, bf16[384,768]{1,0:T(8,128)(2,1)S(1)} %copy-done, bf16[512,384]{1,0:T(8,128)(2,1)S(1)} %bitcast.29, s32[]{:T(128)S(6)} %select_n.21), kind=kOutput, calls=%fused_computation.13 | convolution fusion | flops 152174592 | bytes 1966084 | tf_op jit(solution)/shard_map/dot_general | solution.py:72
  24.7 0.2 pad_maximum_fusion
  24.8 14.4 %all_to_all.33 = f16[4,64,1536]{2,1,0:T(8,128)(2,1)S(1)} all-to-all(f16[4,64,1536]{2,1,0:T(8,128)(2,1)S(1)} %bitcast.22), channel_id=1, replica_groups=mesh['x'=4,'zh'=4,'core'=2,'zl'=4,'y'=8] {'x'}, dimensions={0} | all-to-all | bytes 1572864 | tf_op jit(solution)/shard_map/all_to_all | solution.py:46
  39.3 0.3 fusion
  39.6 20.5 %all_to_all.34 = f16[4,16,1536]{2,1,0:T(8,128)(2,1)S(1)} all-to-all(f16[4,16,1536]{2,1,0:T(8,128)(2,1)S(1)} %multiply_convert_fusion.2), channel_id=1, replica_groups=mesh['x'=4,'zh'=4,'core'=2,'zl'=4,'y'=8] {'zh'}, dimensions={0} | all-to-all | bytes 393216 | tf_op jit(solution)/shard_map/all_to_all | solution.py:46
  60.2 15.4 %all_gather.6 = bf16[64,1536]{1,0:T(8,128)(2,1)S(1)} all-gather(bf16[16,1536]{1,0:T(8,128)(2,1)S(1)} %pad_maximum_fusion.8), channel_id=1, replica_groups=mesh['x'=4,'zh'=4,'core'=2,'zl'=4,'y'=8] {'zh'}, dimensions={0}, use_global_device_ids=true | all-gather | bytes 245760 | tf_op jit(solution)/shard_map/all_gather | solution.py:82
  75.6 10.7 %all_gather.7 = bf16[256,1536]{1,0:T(8,128)(2,1)S(1)} all-gather(bf16[64,1536]{1,0:T(8,128)(2,1)S(1)} %all_gather.6), channel_id=1, replica_groups=mesh['x'=4,'zh'=4,'core'=2,'zl'=4,'y'=8] {'x'}, dimensions={0}, use_global_device_ids=true | all-gather | bytes 983040 | tf_op jit(solution)/shard_map/all_gather | solution.py:83
  86.3 13.8 %collective-permute-start.2 = (bf16[256,1536]{1,0:T(8,128)(2,1)S(1)}, bf16[256,1536]{1,0:T(8,128)(2,1)S(1)}, u32[]{:S(2)}, u32[]{:S(2)}) collective-permute-start(bf16[256,1536]{1,0:T(8,128)(2,1)S(1)} %all_gather.7), channel_id=1, source_target_pairs={{0,32},{32,0},{1,33},{33,1},{2,34},{34,2},{3,35},{35,3},{4,36},{36... | collective-permute-start | bytes 2359304 | tf_op jit(solution)/shard_map/ppermute | solution.py:51
  100.2 1.9 %collective-permute-done.2 = bf16[256,1536]{1,0:T(8,128)(2,1)S(1)} collective-permute-done((bf16[256,1536]{1,0:T(8,128)(2,1)S(1)}, bf16[256,1536]{1,0:T(8,128)(2,1)S(1)}, u32[]{:S(2)}, u32[]{:S(2)}) %collective-permute-start.2) | collective-permute-done | bytes 786464 | tf_op jit(solution)/shard_map/ppermute | solution.py:51
  102.0 0.1 broadcast_select_fusion.1
  102.3 0.5 convolution_convert_fusion
  102.8 0.2 copy-done.6
  103.0 0.1 copy-done.8
  103.1 0.1 copy-done.2
  103.3 0.1 copy-done.4
  103.4 0.5 convolution_convert_fusion.1
  104.0 0.3 copy.17
  104.3 29.5 %all_to_all.35 = bf16[8,64,768]{2,1,0:T(8,128)(2,1)S(1)} all-to-all(bf16[8,64,768]{2,1,0:T(8,128)(2,1)S(1)} %bitcast.23), channel_id=1, replica_groups=mesh['x'=4,'zh'=4,'core'=2,'zl'=4,'y'=8] {'y'}, dimensions={0} | all-to-all | bytes 1572864 | tf_op jit(solution)/shard_map/all_to_all | solution.py:46
  133.8 0.8 convert_reduce_fusion
  134.6 3.4 %all-to-all-start.3 = ((f32[4,16,768]{2,1,0:T(8,128)}), f32[4,16,768]{2,1,0:T(8,128)S(1)}, u32[]{:S(2)}, u32[]{:S(2)}) async-start(f32[4,16,768]{2,1,0:T(8,128)} %bitcast.9), calls=%async_computation.3 | async-start | bytes 393216 | tf_op jit(solution)/shard_map/all_to_all | solution.py:46
  138.0 0.6 convolution_bitcast_fusion
  138.6 1.4 copy.18
  140.0 1.6 %fusion.1 = f32[768,384]{1,0:T(8,128)} fusion(bf16[512,384]{1,0:T(8,128)(2,1)S(1)} %bitcast.27, bf16[256,768]{1,0:T(8,128)(2,1)S(1)} %copy-done.5, bf16[256,768]{1,0:T(8,128)(2,1)S(1)} %copy-done.3), kind=kOutput, calls=%fused_computation.17 | convolution fusion | flops 303562752 | bytes 2359296 | tf_op jit(solution)/shard_map/dot_general | solution.py:40
  141.6 1.4 %all-to-all-done.3 = f32[4,16,768]{2,1,0:T(8,128)S(1)} async-done(((f32[4,16,768]{2,1,0:T(8,128)}), f32[4,16,768]{2,1,0:T(8,128)S(1)}, u32[]{:S(2)}, u32[]{:S(2)}) %all-to-all-start.3) | async-done | bytes 196640 | tf_op jit(solution)/shard_map/all_to_all | solution.py:46
  143.1 0.6 fusion.24
  (27 shorter events, 0.5 us)
Async XLA Ops:
  0.6 17.8 %copy-start = (bf16[384,768]{1,0:T(8,128)(2,1)S(1)}, bf16[384,768]{1,0:T(8,128)(2,1)}, u32[]{:S(2)}) copy-start(bf16[384,768]{1,0:T(8,128)(2,1)} %param.6) | copy-start | bytes 1769476
  0.6 1.2 copy-start.1
  0.7 17.7 %copy-start.10 = (bf16[512,384]{1,0:T(8,128)(2,1)S(1)}, bf16[512,384]{1,0:T(8,128)(2,1)}, u32[]{:S(2)}) copy-start(bf16[512,384]{1,0:T(8,128)(2,1)} %param.4) | copy-start | bytes 1179652
  2.3 18.4 %collective-permute-start.1 = (f32[256,768]{1,0:T(8,128)S(1)}, f32[256,768]{1,0:T(8,128)}, u32[]{:S(2)}, u32[]{:S(2)}) collective-permute-start(f32[256,768]{1,0:T(8,128)S(1)} %fusion.3), channel_id=1, source_target_pairs={{0,32},{32,0},{1,33},{33,1},{2,34},{34,2},{3,35},{35,3},{4,36},{36... | collective-permute-start | bytes 2359304 | tf_op jit(solution)/shard_map/ppermute | solution.py:51
  18.8 4.3 %collective-permute-start = (f32[256,768]{1,0:T(8,128)S(1)}, f32[256,768]{1,0:T(8,128)}, u32[]{:S(2)}, u32[]{:S(2)}) collective-permute-start(f32[256,768]{1,0:T(8,128)S(1)} %fusion.6), channel_id=1, source_target_pairs={{0,32},{32,0},{1,33},{33,1},{2,34},{34,2},{3,35},{35,3},{4,36},{36... | collective-permute-start | bytes 2359304 | tf_op jit(solution)/shard_map/ppermute | solution.py:51
  86.3 15.7 %collective-permute-start.2 = (bf16[256,1536]{1,0:T(8,128)(2,1)S(1)}, bf16[256,1536]{1,0:T(8,128)(2,1)S(1)}, u32[]{:S(2)}, u32[]{:S(2)}) collective-permute-start(bf16[256,1536]{1,0:T(8,128)(2,1)S(1)} %all_gather.7), channel_id=1, source_target_pairs={{0,32},{32,0},{1,33},{33,1},{2,34},{34,2},{3,35},{35,3},{4,36},{36... | collective-permute-start | bytes 2359304 | tf_op jit(solution)/shard_map/ppermute | solution.py:51
  102.3 0.7 copy-start.6
  102.3 0.9 copy-start.8
  102.3 1.0 copy-start.2
  102.3 1.1 copy-start.4
  104.3 33.7 %copy-start.7 = (bf16[256,768]{1,0:T(8,128)(2,1)S(1)}, bf16[256,768]{1,0:T(8,128)(2,1)}, u32[]{:S(2)}) copy-start(bf16[256,768]{1,0:T(8,128)(2,1)} %copy-done.6) | copy-start | bytes 1179652
  104.3 33.7 %copy-start.9 = (bf16[256,768]{1,0:T(8,128)(2,1)S(1)}, bf16[256,768]{1,0:T(8,128)(2,1)}, u32[]{:S(2)}) copy-start(bf16[256,768]{1,0:T(8,128)(2,1)} %copy-done.8) | copy-start | bytes 1179652
  134.6 8.5 %all-to-all-start.3 = ((f32[4,16,768]{2,1,0:T(8,128)}), f32[4,16,768]{2,1,0:T(8,128)S(1)}, u32[]{:S(2)}, u32[]{:S(2)}) async-start(f32[4,16,768]{2,1,0:T(8,128)} %bitcast.9), calls=%async_computation.3 | async-start | bytes 393216 | tf_op jit(solution)/shard_map/all_to_all | solution.py:46
  138.6 1.4 copy-start.3
  138.6 1.4 copy-start.5

commit v2 on v1

--- a/solution.py
+++ b/solution.py
@@ -8,6 +8,8 @@
 
 root_scale = 512.0
 smallest = 1e-37
+
+fourth_scale = 2048.0
 
 
 def gelu_value(pre):
@@ -28,6 +30,18 @@
 def from_root(root):
     root = root.astype(jnp.float32) * (1.0 / root_scale)
     return root * jnp.abs(root)
+
+
+def to_fourth_root(value):
+    size = jnp.maximum(jnp.abs(value), smallest)
+    square = size * lax.rsqrt(size)
+    root = square * lax.rsqrt(square) * fourth_scale
+    return jnp.where(value < 0.0, -root, root).astype(jnp.float16)
+
+
+def from_fourth_root(root):
+    root = root.astype(jnp.float32) * (1.0 / fourth_scale)
+    return root * jnp.abs(root) * (root * root)
 
 
 def contract_last(left, right):
@@ -56,10 +70,10 @@
     hidden = w_in.shape[1]
     half = total // 2
     core = lax.axis_index("core")
-    zl, ny = lax.axis_size("zl"), lax.axis_size("y")
 
     def reorder(array):
-        return array.reshape(zl, ny, -1, features).transpose(1, 0, 2, 3).reshape(total, features)
+        blocks = array.reshape(2, 2, 4, 2, -1, features)
+        return blocks.transpose(1, 3, 0, 2, 4, 5).reshape(total, features)
 
     inputs, cotangent = reorder(inputs), reorder(cotangent)
     in_mine = lax.dynamic_slice(inputs, (core * half, 0), (half, features))
@@ -90,16 +104,18 @@
     out = jnp.dot(act, w_out, preferred_element_type=jnp.float32)
     back = contract_last(pre_grad, w_in)
     sums = jnp.concatenate([out.astype(jnp.bfloat16), back.astype(jnp.bfloat16)], axis=1)
-    sums = jnp.sum(exchange(sums, "y").astype(jnp.float32), axis=0)
-    sums = jnp.sum(exchange(sums, "zl"), axis=0)
+    sums = jnp.sum(exchange(sums, ("zb", "yb")).astype(jnp.float32), axis=0)
+    sums = exchange(to_fourth_root(sums), ("za", "ya"))
+    sums = jnp.sum(from_fourth_root(sums), axis=0)
     w_out_grad = contract_first(act, cotangent)
     w_in_grad = contract_first(inputs, pre_grad)
     return (sums[:, :features], sums[:, features:], w_in_grad, w_out_grad)
 
 
 def solution(mesh):
-    fine = Mesh(mesh.devices.reshape(4, 4, 2, 4, 8), ("x", "zh", "core", "zl", "y"))
-    row, col = ("x", "zh", "core"), ("zl", "y")
+    axes = ("x", "zh", "core", "za", "zb", "ya", "yb")
+    fine = Mesh(mesh.devices.reshape(4, 4, 2, 2, 2, 4, 2), axes)
+    row, col = axes[:3], axes[3:]
     in_specs = (P(None, row), P(None, row), P(row, col), P(col, row))
     out_specs = (P(col, row), P(col, row), P(row, col), P(col, row))
     return jax.shard_map(shards, mesh=fine, in_specs=in_specs, out_specs=out_specs, check_vma=False)

time: 145 us -> 139 us (0.959)
  blocking collectives: 90.5 us -> 73.6 us
  starting transfers between devices: 35.2 us -> 40.5 us
  waiting for transfers between devices: 4.13 us -> 8.11 us
    all_to_all x3, blocking collectives: 64.4 us -> 47.5 us  [exchange(): pieces = lax.all_to_all(value, axis, 0, 0, tiled=True)]
    all_to_all x1, starting transfers between devices: 3.36 us -> 8.66 us  [exchange(): pieces = lax.all_to_all(value, axis, 0, 0, tiled=True)]
    all_to_all x1, waiting for transfers between devices: 1.45 us -> 5.43 us  [exchange(): pieces = lax.all_to_all(value, axis, 0, 0, tiled=True)]
where the time goes in v2:
time: 139 us; the launch traced here: 137 us
  blocking collectives  73.6 us (53%)
  starting transfers between devices  40.5 us (29%)
  waiting for transfers between devices  8.11 us (6%)
  matrix products  7.09 us (5%)
  local copies, waits for them, and re-layouts  4.35 us (3%)
  other arithmetic  2.03 us (1%)
    all_to_all x3, blocking collectives, exchange(): pieces = lax.all_to_all(value, axis, 0, 0, tiled=True)  47.5 us
    ppermute x3, starting transfers between devices, swap_core(): return lax.ppermute(value, 'core', [(0, 1), (1, 0)])  31.8 us
    all_gather x1, blocking collectives, shards(): mine = lax.all_gather(mine, 'zh', axis=0, tiled=True)  15.4 us
    all_gather x1, blocking collectives, shards(): mine = lax.all_gather(mine, 'x', axis=0, tiled=True)  10.7 us
    all_to_all x1, starting transfers between devices, exchange(): pieces = lax.all_to_all(value, axis, 0, 0, tiled=True)  8.66 us
    all_to_all x1, waiting for transfers between devices, exchange(): pieces = lax.all_to_all(value, axis, 0, 0, tiled=True)  5.43 us
  transfers between devices with their start and end apart: 4, of which 3 were waited for; matrix products, arithmetic and copies ran while one was open for 4% of the time, Pallas kernels for 0%

profile of v2, /device:TPU:1, one launch (start us, length us, event | category | flops | bytes accessed | tf_op | source)
XLA Modules:
  0.0 136.6 jit_solution(7969024830875694895)
XLA Ops:
  0.7 1.1 copy.26
  1.9 0.4 fusion.7
  2.3 16.1 %collective-permute-start.1 = (f32[256,768]{1,0:T(8,128)S(1)}, f32[256,768]{1,0:T(8,128)}, u32[]{:S(2)}, u32[]{:S(2)}) collective-permute-start(f32[256,768]{1,0:T(8,128)S(1)} %fusion.7), channel_id=1, source_target_pairs={{0,32},{32,0},{1,33},{33,1},{2,34},{34,2},{3,35},{35,3},{4,36},{36... | collective-permute-start | bytes 2359304 | tf_op jit(solution)/shard_map/ppermute | solution.py:65
  18.4 0.4 fusion.10
  18.8 1.9 %collective-permute-start = (f32[256,768]{1,0:T(8,128)S(1)}, f32[256,768]{1,0:T(8,128)}, u32[]{:S(2)}, u32[]{:S(2)}) collective-permute-start(f32[256,768]{1,0:T(8,128)S(1)} %fusion.10), channel_id=1, source_target_pairs={{0,32},{32,0},{1,33},{33,1},{2,34},{34,2},{3,35},{35,3},{4,36},{36... | collective-permute-start | bytes 2359304 | tf_op jit(solution)/shard_map/ppermute | solution.py:65
  20.7 1.6 %multiply_convert_fusion = f16[256,768]{1,0:T(8,128)(2,1)S(1)} fusion(f32[256,768]{1,0:T(8,128)} %collective-permute-done.1, bf16[768,384]{1,0:T(8,128)(2,1)S(1)} %copy-done.1, bf16[512,384]{1,0:T(8,128)(2,1)S(1)} %bitcast.31, s32[]{:T(128)S(6)} %select_n.26), kind=kOutput, calls=%fused_computation.13 | convolution fusion | flops 152174592 | bytes 1966084 | tf_op jit(solution)/shard_map/dot_general | solution.py:48
  22.3 0.8 collective-permute-done
  23.1 1.6 %multiply_convert_fusion.1 = f16[256,768]{1,0:T(8,128)(2,1)S(1)} fusion(f32[256,768]{1,0:T(8,128)} %collective-permute-done, bf16[384,768]{1,0:T(8,128)(2,1)S(1)} %copy-done, bf16[512,384]{1,0:T(8,128)(2,1)S(1)} %bitcast.34, s32[]{:T(128)S(6)} %select_n.26), kind=kOutput, calls=%fused_computation.14 | convolution fusion | flops 152174592 | bytes 1966084 | tf_op jit(solution)/shard_map/dot_general | solution.py:86
  24.7 0.2 pad_maximum_fusion
  24.8 14.4 %all_to_all.30 = f16[4,64,1536]{2,1,0:T(8,128)(2,1)S(1)} all-to-all(f16[4,64,1536]{2,1,0:T(8,128)(2,1)S(1)} %bitcast.27), channel_id=1, replica_groups=mesh['x'=4,'zh'=4,'core'=2,'za'=2,'zb'=2,'ya'=4,'yb'=2] {'x'}, dimensions={0} | all-to-all | bytes 1572864 | tf_op jit(solution)/shard_map/all_to_all | solution.py:60
  39.3 0.3 fusion
  39.6 20.5 %all_to_all.31 = f16[4,16,1536]{2,1,0:T(8,128)(2,1)S(1)} all-to-all(f16[4,16,1536]{2,1,0:T(8,128)(2,1)S(1)} %multiply_convert_fusion.2), channel_id=1, replica_groups=mesh['x'=4,'zh'=4,'core'=2,'za'=2,'zb'=2,'ya'=4,'yb'=2] {'zh'}, dimensions={0} | all-to-all | bytes 393216 | tf_op jit(solution)/shard_map/all_to_all | solution.py:60
  60.2 15.4 %all_gather.6 = bf16[64,1536]{1,0:T(8,128)(2,1)S(1)} all-gather(bf16[16,1536]{1,0:T(8,128)(2,1)S(1)} %pad_maximum_fusion.7), channel_id=1, replica_groups=mesh['x'=4,'zh'=4,'core'=2,'za'=2,'zb'=2,'ya'=4,'yb'=2] {'zh'}, dimensions={0}, use_global_device_ids=true | all-gather | bytes 245760 | tf_op jit(solution)/shard_map/all_gather | solution.py:96
  75.6 10.7 %all_gather.7 = bf16[256,1536]{1,0:T(8,128)(2,1)S(1)} all-gather(bf16[64,1536]{1,0:T(8,128)(2,1)S(1)} %all_gather.6), channel_id=1, replica_groups=mesh['x'=4,'zh'=4,'core'=2,'za'=2,'zb'=2,'ya'=4,'yb'=2] {'x'}, dimensions={0}, use_global_device_ids=true | all-gather | bytes 983040 | tf_op jit(solution)/shard_map/all_gather | solution.py:97
  86.3 13.8 %collective-permute-start.2 = (bf16[256,1536]{1,0:T(8,128)(2,1)S(1)}, bf16[256,1536]{1,0:T(8,128)(2,1)S(1)}, u32[]{:S(2)}, u32[]{:S(2)}) collective-permute-start(bf16[256,1536]{1,0:T(8,128)(2,1)S(1)} %all_gather.7), channel_id=1, source_target_pairs={{0,32},{32,0},{1,33},{33,1},{2,34},{34,2},{3,35},{35,3},{4,36},{36... | collective-permute-start | bytes 2359304 | tf_op jit(solution)/shard_map/ppermute | solution.py:65
  100.2 1.9 %collective-permute-done.2 = bf16[256,1536]{1,0:T(8,128)(2,1)S(1)} collective-permute-done((bf16[256,1536]{1,0:T(8,128)(2,1)S(1)}, bf16[256,1536]{1,0:T(8,128)(2,1)S(1)}, u32[]{:S(2)}, u32[]{:S(2)}) %collective-permute-start.2) | collective-permute-done | bytes 786464 | tf_op jit(solution)/shard_map/ppermute | solution.py:65
  102.3 0.5 convolution_convert_fusion
  102.8 0.2 copy-done.6
  103.0 0.1 copy-done.8
  103.1 0.1 copy-done.2
  103.4 0.5 convolution_convert_fusion.1
  103.9 0.1 copy_bitcast_fusion
  104.1 12.7 %all_to_all.32 = bf16[4,128,768]{1,2,0:T(8,128)(2,1)S(1)} all-to-all(bf16[4,128,768]{1,2,0:T(8,128)(2,1)S(1)} %copy_bitcast_fusion), channel_id=1, replica_groups=mesh['x'=4,'zh'=4,'core'=2,'za'=2,'zb'=2,'ya'=4,'yb'=2] {'zb','yb'}, dimensions={0} | all-to-all | bytes 1572864 | tf_op jit(solution)/shard_map/all_to_all | solution.py:60
  117.0 0.2 copy.29
  117.2 0.2 copy.30
  117.4 0.8 fusion.4
  118.2 8.7 %all-to-all-start.3 = ((f16[8,16,768]{2,1,0:T(8,128)(2,1)}), f16[8,16,768]{2,1,0:T(8,128)(2,1)S(1)}, u32[]{:S(2)}, u32[]{:S(2)}) async-start(f16[8,16,768]{2,1,0:T(8,128)(2,1)} %fusion.4), calls=%async_computation.3 | async-start | bytes 393216 | tf_op jit(solution)/shard_map/all_to_all | solution.py:60
  126.9 0.6 convolution_bitcast_fusion
  127.5 1.4 %copy.31 = f32[384,768]{1,0:T(8,128)} copy(f32[384,768]{0,1:T(8,128)S(1)} %convolution_bitcast_fusion) | data formatting | bytes 2359296
  128.9 1.6 %fusion.1 = f32[768,384]{1,0:T(8,128)} fusion(bf16[512,384]{1,0:T(8,128)(2,1)S(1)} %bitcast.32, bf16[256,768]{1,0:T(8,128)(2,1)S(1)} %copy-done.5, bf16[256,768]{1,0:T(8,128)(2,1)S(1)} %copy-done.3), kind=kOutput, calls=%fused_computation.22 | convolution fusion | flops 303562752 | bytes 2359296 | tf_op jit(solution)/shard_map/dot_general | solution.py:54
  130.5 5.4 %all-to-all-done.3 = f16[8,16,768]{2,1,0:T(8,128)(2,1)S(1)} async-done(((f16[8,16,768]{2,1,0:T(8,128)(2,1)}), f16[8,16,768]{2,1,0:T(8,128)(2,1)S(1)}, u32[]{:S(2)}, u32[]{:S(2)}) %all-to-all-start.3) | async-done | bytes 196640 | tf_op jit(solution)/shard_map/all_to_all | solution.py:60
  136.0 0.6 fusion.28
  (31 shorter events, 1.0 us)
Async XLA Ops:
  0.6 17.8 %copy-start = (bf16[384,768]{1,0:T(8,128)(2,1)S(1)}, bf16[384,768]{1,0:T(8,128)(2,1)}, u32[]{:S(2)}) copy-start(bf16[384,768]{1,0:T(8,128)(2,1)} %param.6) | copy-start | bytes 1769476
  0.6 1.2 copy-start.1
  0.7 17.7 %copy-start.10 = (bf16[512,384]{1,0:T(8,128)(2,1)S(1)}, bf16[512,384]{1,0:T(8,128)(2,1)}, u32[]{:S(2)}) copy-start(bf16[512,384]{1,0:T(8,128)(2,1)} %param.4) | copy-start | bytes 1179652
  2.3 18.4 %collective-permute-start.1 = (f32[256,768]{1,0:T(8,128)S(1)}, f32[256,768]{1,0:T(8,128)}, u32[]{:S(2)}, u32[]{:S(2)}) collective-permute-start(f32[256,768]{1,0:T(8,128)S(1)} %fusion.7), channel_id=1, source_target_pairs={{0,32},{32,0},{1,33},{33,1},{2,34},{34,2},{3,35},{35,3},{4,36},{36... | collective-permute-start | bytes 2359304 | tf_op jit(solution)/shard_map/ppermute | solution.py:65
  18.8 4.3 %collective-permute-start = (f32[256,768]{1,0:T(8,128)S(1)}, f32[256,768]{1,0:T(8,128)}, u32[]{:S(2)}, u32[]{:S(2)}) collective-permute-start(f32[256,768]{1,0:T(8,128)S(1)} %fusion.10), channel_id=1, source_target_pairs={{0,32},{32,0},{1,33},{33,1},{2,34},{34,2},{3,35},{35,3},{4,36},{36... | collective-permute-start | bytes 2359304 | tf_op jit(solution)/shard_map/ppermute | solution.py:65
  86.3 15.7 %collective-permute-start.2 = (bf16[256,1536]{1,0:T(8,128)(2,1)S(1)}, bf16[256,1536]{1,0:T(8,128)(2,1)S(1)}, u32[]{:S(2)}, u32[]{:S(2)}) collective-permute-start(bf16[256,1536]{1,0:T(8,128)(2,1)S(1)} %all_gather.7), channel_id=1, source_target_pairs={{0,32},{32,0},{1,33},{33,1},{2,34},{34,2},{3,35},{35,3},{4,36},{36... | collective-permute-start | bytes 2359304 | tf_op jit(solution)/shard_map/ppermute | solution.py:65
  102.3 0.7 copy-start.6
  102.3 0.9 copy-start.8
  102.3 1.0 copy-start.2
  102.3 1.1 copy-start.4
  116.9 9.9 %copy-start.7 = (bf16[256,768]{1,0:T(8,128)(2,1)S(1)}, bf16[256,768]{1,0:T(8,128)(2,1)}, u32[]{:S(2)}) copy-start(bf16[256,768]{1,0:T(8,128)(2,1)} %copy-done.6) | copy-start | bytes 1179652
  117.0 9.9 %copy-start.9 = (bf16[256,768]{1,0:T(8,128)(2,1)S(1)}, bf16[256,768]{1,0:T(8,128)(2,1)}, u32[]{:S(2)}) copy-start(bf16[256,768]{1,0:T(8,128)(2,1)} %copy-done.8) | copy-start | bytes 1179652
  118.2 17.7 %all-to-all-start.3 = ((f16[8,16,768]{2,1,0:T(8,128)(2,1)}), f16[8,16,768]{2,1,0:T(8,128)(2,1)S(1)}, u32[]{:S(2)}, u32[]{:S(2)}) async-start(f16[8,16,768]{2,1,0:T(8,128)(2,1)} %fusion.4), calls=%async_computation.3 | async-start | bytes 393216 | tf_op jit(solution)/shard_map/all_to_all | solution.py:60
  127.5 1.4 %copy-start.3 = (bf16[256,768]{1,0:T(8,128)(2,1)S(1)}, bf16[256,768]{1,0:T(8,128)(2,1)}, u32[]{:S(2)}) copy-start(bf16[256,768]{1,0:T(8,128)(2,1)} %copy-done.2) | copy-start | bytes 1179652
  127.5 1.4 %copy-start.5 = (bf16[256,768]{1,0:T(8,128)(2,1)S(1)}, bf16[256,768]{1,0:T(8,128)(2,1)}, u32[]{:S(2)}) copy-start(bf16[256,768]{1,0:T(8,128)(2,1)} %copy-done.4) | copy-start | bytes 1179652

commit v3 on v2

v3 whole, which is shorter than its diff:
```python
import jax
import jax.numpy as jnp
from jax import lax
from jax.sharding import Mesh, PartitionSpec as P

inv_root_two = 0.7071067811865476
density_scale = 0.3989422804014327

root_scale = 512.0
smallest = 1e-37

fourth_scale = 2048.0


def gelu_value(pre):
    return pre * 0.5 * (1.0 + lax.erf(pre * inv_root_two))


def gelu_slope(pre):
    return 0.5 * (1.0 + lax.erf(pre * inv_root_two)) + pre * density_scale * jnp.exp(
        -0.5 * pre * pre
    )


def signed_root(value):
    return value * lax.rsqrt(jnp.maximum(jnp.abs(value), smallest))


def signed_square(root):
    return root * jnp.abs(root)


def to_root(value):
    return (signed_root(value) * root_scale).astype(jnp.float16)


def from_root(root):
    return signed_square(root.astype(jnp.float32) * (1.0 / root_scale))


def to_fourth_root(value):
    return (signed_root(signed_root(value)) * fourth_scale).astype(jnp.float16)


def from_fourth_root(root):
    return signed_square(signed_square(root.astype(jnp.float32) * (1.0 / fourth_scale)))


def contract_last(left, right):
    return lax.dot_general(
        left, right, (((1,), (1,)), ((), ())), preferred_element_type=jnp.float32
    )


def contract_first(left, right):
    return lax.dot_general(
        left, right, (((0,), (0,)), ((), ())), preferred_element_type=jnp.float32
    )


def exchange(value, axis):
    pieces = lax.all_to_all(value, axis, 0, 0, tiled=True)
    return pieces.reshape(lax.axis_size(axis), -1, value.shape[-1])


def swap_core(value):
    return lax.ppermute(value, "core", [(0, 1), (1, 0)])


def core_order(mine, other, axis):
    first = lax.axis_index("core") == 0
    return jnp.concatenate([jnp.where(first, mine, other), jnp.where(first, other, mine)], axis=axis)


def shards(inputs, cotangent, w_in, w_out):
    total, features = inputs.shape
    hidden = w_in.shape[1]
    half = total // 2
    core = lax.axis_index("core")

    in_mine = lax.dynamic_slice(inputs, (core * half, 0), (half, features))
    in_other = lax.dynamic_slice(inputs, ((1 - core) * half, 0), (half, features))
    ct_mine = lax.dynamic_slice(cotangent, (core * half, 0), (half, features))
    ct_other = lax.dynamic_slice(cotangent, ((1 - core) * half, 0), (half, features))

    pre_sent = swap_core(jnp.dot(in_other, w_in, preferred_element_type=jnp.float32))
    grad_sent = swap_core(contract_last(ct_other, w_out))
    pre = jnp.dot(in_mine, w_in, preferred_element_type=jnp.float32) + pre_sent
    grad = contract_last(ct_mine, w_out) + grad_sent

    both = jnp.concatenate([to_root(pre), to_root(grad)], axis=1)
    both = jnp.sum(from_root(exchange(both, "x")), axis=0)
    both, w_in_late, w_out_late = lax.optimization_barrier((both, w_in, w_out))
    both = exchange(to_root(both), "zh")
    w_in_all = core_order(w_in_late, swap_core(w_in_late), 0)
    w_out_all = core_order(w_out_late, swap_core(w_out_late), 1)
    both = jnp.sum(from_root(both), axis=0)
    pre, grad = both[:, :hidden], both[:, hidden:]
    act = gelu_value(pre).astype(jnp.bfloat16)
    pre_grad = (grad * gelu_slope(pre)).astype(jnp.bfloat16)
    mine = jnp.concatenate([act, pre_grad], axis=1)
    mine = lax.all_gather(mine, "zh", axis=0, tiled=True)
    mine = lax.all_gather(mine, "x", axis=0, tiled=True)

    out = jnp.dot(mine[:, :hidden], w_out_all, preferred_element_type=jnp.float32).astype(jnp.bfloat16)
    back = contract_last(mine[:, hidden:], w_in_all).astype(jnp.bfloat16)
    sums = jnp.concatenate([out[:, :features], back[:, :features]], axis=1)
    sums_next = jnp.concatenate([out[:, features:], back[:, features:]], axis=1)
    sums = jnp.concatenate([sums, sums_next], axis=0).reshape(2, 2, 4, 2, -1, 2 * features)
    sums = sums.transpose(0, 1, 3, 2, 4, 5).reshape(-1, 2 * features)
    sums = exchange(sums, ("core", "zb", "yb"))
    sums = jnp.sum(sums.reshape(2, 4, -1, 2 * features).astype(jnp.float32), axis=1)
    sums = to_fourth_root(sums.reshape(-1, 2 * features))
    sums, mine = lax.optimization_barrier((sums, mine))
    sums = jnp.sum(from_fourth_root(exchange(sums, ("za", "ya"))), axis=0)
    every = core_order(mine, swap_core(mine), 0)
    w_out_grad = contract_first(every[:, :hidden], cotangent)
    w_in_grad = contract_first(inputs, every[:, hidden:])
    return (sums[:, :features], sums[:, features:], w_in_grad, w_out_grad)


def solution(mesh):
    axes = ("x", "zh", "core", "za", "zb", "ya", "yb")
    fine = Mesh(mesh.devices.reshape(4, 4, 2, 2, 2, 4, 2), axes)
    row, col = axes[:3], axes[3:]
    in_specs = (P(None, row), P(None, row), P(row, col), P(col, row))
    out_specs = (P(col, row), P(col, row), P(row, col), P(col, row))
    return jax.shard_map(shards, mesh=fine, in_specs=in_specs, out_specs=out_specs, check_vma=False)
```

time: 139 us -> 138 us (level); the launches traced: 137 us -> 137 us
  waiting for transfers between devices: 8.11 us -> 15.9 us
  blocking collectives: 73.6 us -> 66.9 us
    all_to_all x1 -> x2, waiting for transfers between devices: 5.43 us -> 15.1 us  [exchange(): pieces = lax.all_to_all(value, axis, 0, 0, tiled=True)]
    all_to_all x3 -> x2, blocking collectives: 47.5 us -> 40.8 us  [exchange(): pieces = lax.all_to_all(value, axis, 0, 0, tiled=True)]
    ppermute x3 -> x5, starting transfers between devices: 31.8 us -> 26 us  [swap_core(): return lax.ppermute(value, 'core', [(0, 1), (1, 0)])]
    all_to_all x1 -> x2, starting transfers between devices: 8.66 us -> 13.5 us  [exchange(): pieces = lax.all_to_all(value, axis, 0, 0, tiled=True)]
    ppermute x3 -> x5, waiting for transfers between devices: 2.68 us -> 0.8 us  [swap_core(): return lax.ppermute(value, 'core', [(0, 1), (1, 0)])]
  transfers between devices with their start and end apart: 4 -> 7, of which waited for: 3 -> 3; matrix products, arithmetic and copies ran while one was open for 4% -> 2% of each run, Pallas kernels for 0% -> 0%
where the time goes in v3:
time: 138 us; the launch traced here: 137 us
  blocking collectives  66.9 us (48%)
  starting transfers between devices  39.5 us (29%)
  waiting for transfers between devices  15.9 us (12%)
  matrix products  8.14 us (6%)
  local copies, waits for them, and re-layouts  3.13 us (2%)
  other arithmetic  2.72 us (2%)
    all_to_all x2, blocking collectives, exchange(): pieces = lax.all_to_all(value, axis, 0, 0, tiled=True)  40.8 us
    ppermute x5, starting transfers between devices, swap_core(): return lax.ppermute(value, 'core', [(0, 1), (1, 0)])  26 us
    all_gather x1, blocking collectives, shards(): mine = lax.all_gather(mine, 'zh', axis=0, tiled=True)  15.4 us
    all_to_all x2, waiting for transfers between devices, exchange(): pieces = lax.all_to_all(value, axis, 0, 0, tiled=True)  15.1 us
    all_to_all x2, starting transfers between devices, exchange(): pieces = lax.all_to_all(value, axis, 0, 0, tiled=True)  13.5 us
    all_gather x1, blocking collectives, shards(): mine = lax.all_gather(mine, 'x', axis=0, tiled=True)  10.7 us
    dot_general x3, matrix products, contract_last(): lax.dot_general(left, right, (((1,), (1,)), ((), ())), preferred_element_...  3.52 us
  transfers between devices with their start and end apart: 7, of which 3 were waited for; matrix products, arithmetic and copies ran while one was open for 2% of the time, Pallas kernels for 0%

profile of v3, /device:TPU:1, one launch (start us, length us, event | category | flops | bytes accessed | tf_op | source)
XLA Modules:
  0.0 137.2 jit_solution(5688072017024465126)
XLA Ops:
  0.7 1.0 copy-done
  1.6 1.4 %fusion.17 = f32[256,768]{1,0:T(8,128)S(1)} fusion(bf16[768,384]{1,0:T(8,128)(2,1)} %param.7, bf16[512,384]{1,0:T(8,128)(2,1)S(1)} %copy-done, s32[]{:T(128)S(6)} %select_n.45), kind=kOutput, calls=%fused_computation.43 | convolution fusion | flops 150994944 | bytes 1572868 | tf_op jit(solution)/shard_map/dot_general | solution.py:50
  3.1 16.2 %collective-permute-start.1 = (f32[256,768]{1,0:T(8,128)S(1)}, f32[256,768]{1,0:T(8,128)}, u32[]{:S(2)}, u32[]{:S(2)}) collective-permute-start(f32[256,768]{1,0:T(8,128)S(1)} %fusion.17), channel_id=1, source_target_pairs={{0,32},{32,0},{1,33},{33,1},{2,34},{34,2},{3,35},{35,3},{4,36},{36... | collective-permute-start | bytes 2359304 | tf_op jit(solution)/shard_map/ppermute | solution.py:67
  19.3 0.4 fusion.20
  19.7 1.9 %collective-permute-start = (f32[256,768]{1,0:T(8,128)S(1)}, f32[256,768]{1,0:T(8,128)}, u32[]{:S(2)}, u32[]{:S(2)}) collective-permute-start(f32[256,768]{1,0:T(8,128)S(1)} %fusion.20), channel_id=1, source_target_pairs={{0,32},{32,0},{1,33},{33,1},{2,34},{34,2},{3,35},{35,3},{4,36},{36... | collective-permute-start | bytes 2359304 | tf_op jit(solution)/shard_map/ppermute | solution.py:67
  21.6 1.6 %multiply_convert_fusion = f16[256,768]{1,0:T(8,128)(2,1)S(1)} fusion(f32[256,768]{1,0:T(8,128)} %collective-permute-done.1, bf16[768,384]{1,0:T(8,128)(2,1)S(1)} %copy-done.1, bf16[512,384]{1,0:T(8,128)(2,1)S(1)} %copy-done, s32[]{:T(128)S(6)} %select_n.44), kind=kOutput, calls=%fused_computation.22 | convolution fusion | flops 152174592 | bytes 1966084 | tf_op jit(solution)/shard_map/dot_general | solution.py:50
  23.2 0.8 collective-permute-done
  24.0 1.6 %multiply_convert_fusion.1 = f16[256,768]{1,0:T(8,128)(2,1)S(1)} fusion(f32[256,768]{1,0:T(8,128)} %collective-permute-done, bf16[384,768]{1,0:T(8,128)(2,1)S(1)} %copy-done.2, bf16[512,384]{1,0:T(8,128)(2,1)S(1)} %copy-done.3, s32[]{:T(128)S(6)} %select_n.44), kind=kOutput, calls=%fused_computation.23 | convolution fusion | flops 152174592 | bytes 1966084 | tf_op jit(solution)/shard_map/dot_general | solution.py:88
  25.6 0.2 pad_maximum_fusion.2
  25.7 14.4 %all_to_all.36 = f16[4,64,1536]{2,1,0:T(8,128)(2,1)S(1)} all-to-all(f16[4,64,1536]{2,1,0:T(8,128)(2,1)S(1)} %bitcast.30), channel_id=1, replica_groups=mesh['x'=4,'zh'=4,'core'=2,'za'=2,'zb'=2,'ya'=4,'yb'=2] {'x'}, dimensions={0} | all-to-all | bytes 1572864 | tf_op jit(solution)/shard_map/all_to_all | solution.py:62
  40.2 0.3 fusion
  40.4 0.8 multiply_convert_fusion.3
  41.2 7.2 %all-to-all-start.1 = ((f16[4,16,1536]{2,1,0:T(8,128)(2,1)}), f16[4,16,1536]{2,1,0:T(8,128)(2,1)S(1)}, u32[]{:S(2)}, u32[]{:S(2)}) async-start(f16[4,16,1536]{2,1,0:T(8,128)(2,1)} %bitcast.1), calls=%async_computation.1 | async-start | bytes 393216 | tf_op jit(solution)/shard_map/all_to_all | solution.py:62
  48.4 3.4 %collective-permute-start.2 = (bf16[768,384]{1,0:T(8,128)(2,1)S(1)}, bf16[768,384]{1,0:T(8,128)(2,1)S(1)}, u32[]{:S(2)}, u32[]{:S(2)}) collective-permute-start(bf16[768,384]{1,0:T(8,128)(2,1)S(1)} %copy-done.1), channel_id=1, source_target_pairs={{0,32},{32,0},{1,33},{33,1},{2,34},{34,2},{3,35},{35,3},{4,36},{36... | collective-permute-start | bytes 1769480 | tf_op jit(solution)/shard_map/ppermute | solution.py:67
  51.8 1.9 %collective-permute-start.3 = (bf16[384,768]{1,0:T(8,128)(2,1)S(1)}, bf16[384,768]{1,0:T(8,128)(2,1)S(1)}, u32[]{:S(2)}, u32[]{:S(2)}) collective-permute-start(bf16[384,768]{1,0:T(8,128)(2,1)S(1)} %copy-done.2), channel_id=1, source_target_pairs={{0,32},{32,0},{1,33},{33,1},{2,34},{34,2},{3,35},{35,3},{4,36},{36... | collective-permute-start | bytes 1769480 | tf_op jit(solution)/shard_map/ppermute | solution.py:67
  53.8 7.7 %all-to-all-done.1 = f16[4,16,1536]{2,1,0:T(8,128)(2,1)S(1)} async-done(((f16[4,16,1536]{2,1,0:T(8,128)(2,1)}), f16[4,16,1536]{2,1,0:T(8,128)(2,1)S(1)}, u32[]{:S(2)}, u32[]{:S(2)}) %all-to-all-start.1) | async-done | bytes 196640 | tf_op jit(solution)/shard_map/all_to_all | solution.py:62
  61.6 0.1 broadcast_select_fusion.5
  61.7 15.4 %all_gather.6 = bf16[64,1536]{1,0:T(8,128)(2,1)S(1)} all-gather(bf16[16,1536]{1,0:T(8,128)(2,1)S(1)} %pad_maximum_fusion.3), channel_id=1, replica_groups=mesh['x'=4,'zh'=4,'core'=2,'za'=2,'zb'=2,'ya'=4,'yb'=2] {'zh'}, dimensions={0}, use_global_device_ids=true | all-gather | bytes 245760 | tf_op jit(solution)/shard_map/all_gather | solution.py:102
  77.1 10.7 %all_gather.7 = bf16[256,1536]{1,0:T(8,128)(2,1)S(1)} all-gather(bf16[64,1536]{1,0:T(8,128)(2,1)S(1)} %all_gather.6), channel_id=1, replica_groups=mesh['x'=4,'zh'=4,'core'=2,'za'=2,'zb'=2,'ya'=4,'yb'=2] {'x'}, dimensions={0}, use_global_device_ids=true | all-gather | bytes 983040 | tf_op jit(solution)/shard_map/all_gather | solution.py:103
  87.8 0.5 convolution_convert_fusion.1
  88.4 0.5 convolution_convert_fusion
  89.2 26.4 %all_to_all.37 = bf16[8,64,768]{2,1,0:T(8,128)(2,1)S(1)} all-to-all(bf16[8,64,768]{2,1,0:T(8,128)(2,1)S(1)} %bitcast.31), channel_id=1, replica_groups=mesh['x'=4,'zh'=4,'core'=2,'za'=2,'zb'=2,'ya'=4,'yb'=2] {'core','zb','yb'}, dimensions={0} | all-to-all | bytes 1572864 | tf_op jit(solution)/shard_map/all_to_all | solution.py:62
  115.6 0.1 convert_reduce_fusion
  115.7 0.8 multiply_convert_fusion.2
  116.5 6.3 %all-to-all-start.3 = ((f16[8,16,768]{2,1,0:T(8,128)(2,1)}), f16[8,16,768]{2,1,0:T(8,128)(2,1)S(1)}, u32[]{:S(2)}, u32[]{:S(2)}) async-start(f16[8,16,768]{2,1,0:T(8,128)(2,1)} %bitcast.7), calls=%async_computation.3 | async-start | bytes 393216 | tf_op jit(solution)/shard_map/all_to_all | solution.py:62
  122.8 2.5 %collective-permute-start.4 = (bf16[256,1536]{1,0:T(8,128)(2,1)S(1)}, bf16[256,1536]{1,0:T(8,128)(2,1)S(1)}, u32[]{:S(2)}, u32[]{:S(2)}) collective-permute-start(bf16[256,1536]{1,0:T(8,128)(2,1)S(1)} %all_gather.7), channel_id=1, source_target_pairs={{0,32},{32,0},{1,33},{33,1},{2,34},{34,2},{3,35},{35,3},{4,36},{36... | collective-permute-start | bytes 2359304 | tf_op jit(solution)/shard_map/ppermute | solution.py:67
  125.4 7.3 %all-to-all-done.3 = f16[8,16,768]{2,1,0:T(8,128)(2,1)S(1)} async-done(((f16[8,16,768]{2,1,0:T(8,128)(2,1)}), f16[8,16,768]{2,1,0:T(8,128)(2,1)S(1)}, u32[]{:S(2)}, u32[]{:S(2)}) %all-to-all-start.3) | async-done | bytes 196640 | tf_op jit(solution)/shard_map/all_to_all | solution.py:62
  132.8 0.6 fusion.38
  133.4 0.1 broadcast_select_fusion
  133.5 1.6 %fusion.9 = f32[768,384]{1,0:T(8,128)} fusion(bf16[512,384]{1,0:T(8,128)(2,1)S(1)} %copy-done, bf16[256,1536]{1,0:T(8,128)(2,1)S(1)} %get-tuple-element.26, bf16[256,1536]{1,0:T(8,128)(2,1)S(1)} %get-tuple-element.27), kind=kOutput, calls=%fused_computation.18 | convolution fusion | flops 303562752 | bytes 3145728 | tf_op jit(solution)/shard_map/dot_general | solution.py:56
  135.2 0.6 convolution_bitcast_fusion
  135.8 1.4 %copy.12 = f32[384,768]{1,0:T(8,128)} copy(f32[384,768]{0,1:T(8,128)S(1)} %convolution_bitcast_fusion) | data formatting | bytes 2359296
  (19 shorter events, 0.5 us)
Async XLA Ops:
  0.6 1.0 copy-start
  0.6 18.7 %copy-start.2 = (bf16[384,768]{1,0:T(8,128)(2,1)S(1)}, bf16[384,768]{1,0:T(8,128)(2,1)}, u32[]{:S(2)}) copy-start(bf16[384,768]{1,0:T(8,128)(2,1)} %param.6) | copy-start | bytes 1769476
  0.7 18.7 %copy-start.3 = (bf16[512,384]{1,0:T(8,128)(2,1)S(1)}, bf16[512,384]{1,0:T(8,128)(2,1)}, u32[]{:S(2)}) copy-start(bf16[512,384]{1,0:T(8,128)(2,1)} %param.4) | copy-start | bytes 1179652
  3.1 18.5 %copy-start.1 = (bf16[768,384]{1,0:T(8,128)(2,1)S(1)}, bf16[768,384]{1,0:T(8,128)(2,1)}, u32[]{:S(2)}) copy-start(bf16[768,384]{1,0:T(8,128)(2,1)} %param.7) | copy-start | bytes 1769476
  3.1 18.5 %collective-permute-start.1 = (f32[256,768]{1,0:T(8,128)S(1)}, f32[256,768]{1,0:T(8,128)}, u32[]{:S(2)}, u32[]{:S(2)}) collective-permute-start(f32[256,768]{1,0:T(8,128)S(1)} %fusion.17), channel_id=1, source_target_pairs={{0,32},{32,0},{1,33},{33,1},{2,34},{34,2},{3,35},{35,3},{4,36},{36... | collective-permute-start | bytes 2359304 | tf_op jit(solution)/shard_map/ppermute | solution.py:67
  19.7 4.3 %collective-permute-start = (f32[256,768]{1,0:T(8,128)S(1)}, f32[256,768]{1,0:T(8,128)}, u32[]{:S(2)}, u32[]{:S(2)}) collective-permute-start(f32[256,768]{1,0:T(8,128)S(1)} %fusion.20), channel_id=1, source_target_pairs={{0,32},{32,0},{1,33},{33,1},{2,34},{34,2},{3,35},{35,3},{4,36},{36... | collective-permute-start | bytes 2359304 | tf_op jit(solution)/shard_map/ppermute | solution.py:67
  41.2 20.3 %all-to-all-start.1 = ((f16[4,16,1536]{2,1,0:T(8,128)(2,1)}), f16[4,16,1536]{2,1,0:T(8,128)(2,1)S(1)}, u32[]{:S(2)}, u32[]{:S(2)}) async-start(f16[4,16,1536]{2,1,0:T(8,128)(2,1)} %bitcast.1), calls=%async_computation.1 | async-start | bytes 393216 | tf_op jit(solution)/shard_map/all_to_all | solution.py:62
  48.4 13.3 %collective-permute-start.2 = (bf16[768,384]{1,0:T(8,128)(2,1)S(1)}, bf16[768,384]{1,0:T(8,128)(2,1)S(1)}, u32[]{:S(2)}, u32[]{:S(2)}) collective-permute-start(bf16[768,384]{1,0:T(8,128)(2,1)S(1)} %copy-done.1), channel_id=1, source_target_pairs={{0,32},{32,0},{1,33},{33,1},{2,34},{34,2},{3,35},{35,3},{4,36},{36... | collective-permute-start | bytes 1769480 | tf_op jit(solution)/shard_map/ppermute | solution.py:67
  51.8 36.5 %collective-permute-start.3 = (bf16[384,768]{1,0:T(8,128)(2,1)S(1)}, bf16[384,768]{1,0:T(8,128)(2,1)S(1)}, u32[]{:S(2)}, u32[]{:S(2)}) collective-permute-start(bf16[384,768]{1,0:T(8,128)(2,1)S(1)} %copy-done.2), channel_id=1, source_target_pairs={{0,32},{32,0},{1,33},{33,1},{2,34},{34,2},{3,35},{35,3},{4,36},{36... | collective-permute-start | bytes 1769480 | tf_op jit(solution)/shard_map/ppermute | solution.py:67
  116.5 16.2 %all-to-all-start.3 = ((f16[8,16,768]{2,1,0:T(8,128)(2,1)}), f16[8,16,768]{2,1,0:T(8,128)(2,1)S(1)}, u32[]{:S(2)}, u32[]{:S(2)}) async-start(f16[8,16,768]{2,1,0:T(8,128)(2,1)} %bitcast.7), calls=%async_computation.3 | async-start | bytes 393216 | tf_op jit(solution)/shard_map/all_to_all | solution.py:62
  122.8 10.6 %collective-permute-start.4 = (bf16[256,1536]{1,0:T(8,128)(2,1)S(1)}, bf16[256,1536]{1,0:T(8,128)(2,1)S(1)}, u32[]{:S(2)}, u32[]{:S(2)}) collective-permute-start(bf16[256,1536]{1,0:T(8,128)(2,1)S(1)} %all_gather.7), channel_id=1, source_target_pairs={{0,32},{32,0},{1,33},{33,1},{2,34},{34,2},{3,35},{35,3},{4,36},{36... | collective-permute-start | bytes 2359304 | tf_op jit(solution)/shard_map/ppermute | solution.py:67

commit v4 on v3

--- a/solution.py
+++ b/solution.py
@@ -111,11 +111,11 @@
     sums = exchange(sums, ("core", "zb", "yb"))
     sums = jnp.sum(sums.reshape(2, 4, -1, 2 * features).astype(jnp.float32), axis=1)
     sums = to_fourth_root(sums.reshape(-1, 2 * features))
-    sums, mine = lax.optimization_barrier((sums, mine))
-    sums = jnp.sum(from_fourth_root(exchange(sums, ("za", "ya"))), axis=0)
     every = core_order(mine, swap_core(mine), 0)
     w_out_grad = contract_first(every[:, :hidden], cotangent)
     w_in_grad = contract_first(inputs, every[:, hidden:])
+    sums, w_out_grad, w_in_grad = lax.optimization_barrier((sums, w_out_grad, w_in_grad))
+    sums = jnp.sum(from_fourth_root(exchange(sums, ("za", "ya"))), axis=0)
     return (sums[:, :features], sums[:, features:], w_in_grad, w_out_grad)
 
 

time: 138 us -> 136 us (0.986)
  blocking collectives: 66.9 us -> 40.5 us
  starting transfers between devices: 39.5 us -> 54.1 us
  waiting for transfers between devices: 15.9 us -> 26.1 us
    all_to_all x2 -> x1, blocking collectives: 40.8 us -> 14.4 us  [exchange(): pieces = lax.all_to_all(value, axis, 0, 0, tiled=True)]
    all_to_all x2 -> x3, starting transfers between devices: 13.5 us -> 28.7 us  [exchange(): pieces = lax.all_to_all(value, axis, 0, 0, tiled=True)]
    all_to_all x2 -> x3, waiting for transfers between devices: 15.1 us -> 23.1 us  [exchange(): pieces = lax.all_to_all(value, axis, 0, 0, tiled=True)]
    ppermute x5, waiting for transfers between devices: 0.8 us -> 3.03 us  [swap_core(): return lax.ppermute(value, 'core', [(0, 1), (1, 0)])]
  transfers between devices with their start and end apart: 7 -> 8, of which waited for: 3 -> 5; matrix products, arithmetic and copies ran while one was open for 2% -> 5% of each run, Pallas kernels for 0% -> 0%
where the time goes in v4:
time: 136 us
  starting transfers between devices  54.1 us (40%)
  blocking collectives  40.5 us (30%)
  waiting for transfers between devices  26.1 us (19%)
  matrix products  8.33 us (6%)
  local copies, waits for them, and re-layouts  3.06 us (2%)
  other arithmetic  2.81 us (2%)
    all_to_all x3, starting transfers between devices, exchange(): pieces = lax.all_to_all(value, axis, 0, 0, tiled=True)  28.7 us
    ppermute x5, starting transfers between devices, swap_core(): return lax.ppermute(value, 'core', [(0, 1), (1, 0)])  25.4 us
    all_to_all x3, waiting for transfers between devices, exchange(): pieces = lax.all_to_all(value, axis, 0, 0, tiled=True)  23.1 us
    all_gather x1, blocking collectives, shards(): mine = lax.all_gather(mine, 'zh', axis=0, tiled=True)  15.4 us
    all_to_all x1, blocking collectives, exchange(): pieces = lax.all_to_all(value, axis, 0, 0, tiled=True)  14.4 us
    all_gather x1, blocking collectives, shards(): mine = lax.all_gather(mine, 'x', axis=0, tiled=True)  10.7 us
    dot_general x3, matrix products, contract_last(): lax.dot_general(left, right, (((1,), (1,)), ((), ())), preferred_element_...  3.7 us
    ppermute x5, waiting for transfers between devices, swap_core(): return lax.ppermute(value, 'core', [(0, 1), (1, 0)])  3.03 us
  transfers between devices with their start and end apart: 8, of which 5 were waited for; matrix products, arithmetic and copies ran while one was open for 5% of the time, Pallas kernels for 0%

profile of v4, /device:TPU:1, one launch (start us, length us, event | category | flops | bytes accessed | tf_op | source)
XLA Modules:
  0.0 135.8 jit_solution(16477257400867629434)
XLA Ops:
  0.7 1.6 %fusion.17 = f32[256,768]{1,0:T(8,128)S(1)} fusion(bf16[768,384]{1,0:T(8,128)(2,1)} %param.7, bf16[512,384]{1,0:T(8,128)(2,1)} %param.5, s32[]{:T(128)S(6)} %select_n.45), kind=kOutput, calls=%fused_computation.43 | convolution fusion | flops 150994944 | bytes 1572868 | tf_op jit(solution)/shard_map/dot_general | solution.py:50
  2.3 16.2 %collective-permute-start.1 = (f32[256,768]{1,0:T(8,128)S(1)}, f32[256,768]{1,0:T(8,128)}, u32[]{:S(2)}, u32[]{:S(2)}) collective-permute-start(f32[256,768]{1,0:T(8,128)S(1)} %fusion.17), channel_id=1, source_target_pairs={{0,32},{32,0},{1,33},{33,1},{2,34},{34,2},{3,35},{35,3},{4,36},{36... | collective-permute-start | bytes 2359304 | tf_op jit(solution)/shard_map/ppermute | solution.py:67
  18.5 0.4 fusion.20
  18.9 1.9 %collective-permute-start = (f32[256,768]{1,0:T(8,128)S(1)}, f32[256,768]{1,0:T(8,128)}, u32[]{:S(2)}, u32[]{:S(2)}) collective-permute-start(f32[256,768]{1,0:T(8,128)S(1)} %fusion.20), channel_id=1, source_target_pairs={{0,32},{32,0},{1,33},{33,1},{2,34},{34,2},{3,35},{35,3},{4,36},{36... | collective-permute-start | bytes 2359304 | tf_op jit(solution)/shard_map/ppermute | solution.py:67
  20.9 1.6 %multiply_convert_fusion = f16[256,768]{1,0:T(8,128)(2,1)S(1)} fusion(f32[256,768]{1,0:T(8,128)} %collective-permute-done.1, bf16[768,384]{1,0:T(8,128)(2,1)S(1)} %copy-done.1, bf16[512,384]{1,0:T(8,128)(2,1)S(1)} %copy-done.3, s32[]{:T(128)S(6)} %select_n.44), kind=kOutput, calls=%fused_computation.22 | convolution fusion | flops 152174592 | bytes 1966084 | tf_op jit(solution)/shard_map/dot_general | solution.py:50
  22.4 0.8 collective-permute-done
  23.2 1.6 %multiply_convert_fusion.1 = f16[256,768]{1,0:T(8,128)(2,1)S(1)} fusion(f32[256,768]{1,0:T(8,128)} %collective-permute-done, bf16[384,768]{1,0:T(8,128)(2,1)S(1)} %copy-done.2, bf16[512,384]{1,0:T(8,128)(2,1)S(1)} %copy-done, s32[]{:T(128)S(6)} %select_n.44), kind=kOutput, calls=%fused_computation.23 | convolution fusion | flops 152174592 | bytes 1966084 | tf_op jit(solution)/shard_map/dot_general | solution.py:88
  24.8 0.2 pad_maximum_fusion.2
  25.0 14.4 %all_to_all.36 = f16[4,64,1536]{2,1,0:T(8,128)(2,1)S(1)} all-to-all(f16[4,64,1536]{2,1,0:T(8,128)(2,1)S(1)} %bitcast.30), channel_id=1, replica_groups=mesh['x'=4,'zh'=4,'core'=2,'za'=2,'zb'=2,'ya'=4,'yb'=2] {'x'}, dimensions={0} | all-to-all | bytes 1572864 | tf_op jit(solution)/shard_map/all_to_all | solution.py:62
  39.4 0.3 fusion
  39.6 0.8 multiply_convert_fusion.3
  40.4 7.2 %all-to-all-start.1 = ((f16[4,16,1536]{2,1,0:T(8,128)(2,1)}), f16[4,16,1536]{2,1,0:T(8,128)(2,1)S(1)}, u32[]{:S(2)}, u32[]{:S(2)}) async-start(f16[4,16,1536]{2,1,0:T(8,128)(2,1)} %bitcast.1), calls=%async_computation.1 | async-start | bytes 393216 | tf_op jit(solution)/shard_map/all_to_all | solution.py:62
  47.6 3.4 %collective-permute-start.2 = (bf16[768,384]{1,0:T(8,128)(2,1)S(1)}, bf16[768,384]{1,0:T(8,128)(2,1)S(1)}, u32[]{:S(2)}, u32[]{:S(2)}) collective-permute-start(bf16[768,384]{1,0:T(8,128)(2,1)S(1)} %copy-done.1), channel_id=1, source_target_pairs={{0,32},{32,0},{1,33},{33,1},{2,34},{34,2},{3,35},{35,3},{4,36},{36... | collective-permute-start | bytes 1769480 | tf_op jit(solution)/shard_map/ppermute | solution.py:67
  51.0 1.9 %collective-permute-start.3 = (bf16[384,768]{1,0:T(8,128)(2,1)S(1)}, bf16[384,768]{1,0:T(8,128)(2,1)S(1)}, u32[]{:S(2)}, u32[]{:S(2)}) collective-permute-start(bf16[384,768]{1,0:T(8,128)(2,1)S(1)} %copy-done.2), channel_id=1, source_target_pairs={{0,32},{32,0},{1,33},{33,1},{2,34},{34,2},{3,35},{35,3},{4,36},{36... | collective-permute-start | bytes 1769480 | tf_op jit(solution)/shard_map/ppermute | solution.py:67
  53.0 7.7 %all-to-all-done.1 = f16[4,16,1536]{2,1,0:T(8,128)(2,1)S(1)} async-done(((f16[4,16,1536]{2,1,0:T(8,128)(2,1)}), f16[4,16,1536]{2,1,0:T(8,128)(2,1)S(1)}, u32[]{:S(2)}, u32[]{:S(2)}) %all-to-all-start.1) | async-done | bytes 196640 | tf_op jit(solution)/shard_map/all_to_all | solution.py:62
  61.0 15.4 %all_gather.6 = bf16[64,1536]{1,0:T(8,128)(2,1)S(1)} all-gather(bf16[16,1536]{1,0:T(8,128)(2,1)S(1)} %pad_maximum_fusion.3), channel_id=1, replica_groups=mesh['x'=4,'zh'=4,'core'=2,'za'=2,'zb'=2,'ya'=4,'yb'=2] {'zh'}, dimensions={0}, use_global_device_ids=true | all-gather | bytes 245760 | tf_op jit(solution)/shard_map/all_gather | solution.py:102
  76.3 10.7 %all_gather.7 = bf16[256,1536]{1,0:T(8,128)(2,1)S(1)} all-gather(bf16[64,1536]{1,0:T(8,128)(2,1)S(1)} %all_gather.6), channel_id=1, replica_groups=mesh['x'=4,'zh'=4,'core'=2,'za'=2,'zb'=2,'ya'=4,'yb'=2] {'x'}, dimensions={0}, use_global_device_ids=true | all-gather | bytes 983040 | tf_op jit(solution)/shard_map/all_gather | solution.py:103
  87.1 0.5 convolution_convert_fusion.1
  87.6 0.5 convolution_convert_fusion
  88.3 0.9 copy.11
  89.3 14.8 %all-to-all-start.2 = ((bf16[8,64,768]{2,1,0:T(8,128)(2,1)}), bf16[8,64,768]{2,1,0:T(8,128)(2,1)S(1)}, u32[]{:S(2)}, u32[]{:S(2)}) async-start(bf16[8,64,768]{2,1,0:T(8,128)(2,1)} %bitcast.4), calls=%async_computation.2 | async-start | bytes 1572864 | tf_op jit(solution)/shard_map/all_to_all | solution.py:62
  104.0 1.9 %collective-permute-start.4 = (bf16[256,1536]{1,0:T(8,128)(2,1)S(1)}, bf16[256,1536]{1,0:T(8,128)(2,1)S(1)}, u32[]{:S(2)}, u32[]{:S(2)}) collective-permute-start(bf16[256,1536]{1,0:T(8,128)(2,1)S(1)} %all_gather.7), channel_id=1, source_target_pairs={{0,32},{32,0},{1,33},{33,1},{2,34},{34,2},{3,35},{35,3},{4,36},{36... | collective-permute-start | bytes 2359304 | tf_op jit(solution)/shard_map/ppermute | solution.py:67
  106.0 2.3 %collective-permute-done.4 = bf16[256,1536]{1,0:T(8,128)(2,1)S(1)} collective-permute-done((bf16[256,1536]{1,0:T(8,128)(2,1)S(1)}, bf16[256,1536]{1,0:T(8,128)(2,1)S(1)}, u32[]{:S(2)}, u32[]{:S(2)}) %collective-permute-start.4) | collective-permute-done | bytes 786464 | tf_op jit(solution)/shard_map/ppermute | solution.py:67
  108.2 0.2 broadcast_select_fusion
  108.4 0.6 convolution_bitcast_fusion
  109.0 1.6 %fusion.8 = f32[768,384]{1,0:T(8,128)} fusion(bf16[512,384]{1,0:T(8,128)(2,1)S(1)} %copy-done.3, bf16[256,1536]{1,0:T(8,128)(2,1)S(1)} %get-tuple-element.29, bf16[256,1536]{1,0:T(8,128)(2,1)S(1)} %get-tuple-element.28), kind=kOutput, calls=%fused_computation.17 | convolution fusion | flops 303562752 | bytes 3145728 | tf_op jit(solution)/shard_map/dot_general | solution.py:56
  110.6 5.3 %all-to-all-done.2 = bf16[8,64,768]{2,1,0:T(8,128)(2,1)S(1)} async-done(((bf16[8,64,768]{2,1,0:T(8,128)(2,1)}), bf16[8,64,768]{2,1,0:T(8,128)(2,1)S(1)}, u32[]{:S(2)}, u32[]{:S(2)}) %all-to-all-start.2) | async-done | bytes 786464 | tf_op jit(solution)/shard_map/all_to_all | solution.py:62
  116.0 0.8 multiply_convert_fusion.2
  116.8 6.8 %all-to-all-start.3 = ((f16[8,16,768]{2,1,0:T(8,128)(2,1)}), f16[8,16,768]{2,1,0:T(8,128)(2,1)S(1)}, u32[]{:S(2)}, u32[]{:S(2)}) async-start(f16[8,16,768]{2,1,0:T(8,128)(2,1)} %bitcast.8), calls=%async_computation.3 | async-start | bytes 393216 | tf_op jit(solution)/shard_map/all_to_all | solution.py:62
  123.6 1.4 %copy.12 = f32[384,768]{1,0:T(8,128)} copy(f32[384,768]{0,1:T(8,128)S(1)} %convolution_bitcast_fusion) | data formatting | bytes 2359296
  125.0 10.1 %all-to-all-done.3 = f16[8,16,768]{2,1,0:T(8,128)(2,1)S(1)} async-done(((f16[8,16,768]{2,1,0:T(8,128)(2,1)}), f16[8,16,768]{2,1,0:T(8,128)(2,1)S(1)}, u32[]{:S(2)}, u32[]{:S(2)}) %all-to-all-start.3) | async-done | bytes 196640 | tf_op jit(solution)/shard_map/all_to_all | solution.py:62
  135.2 0.6 fusion.38
  (20 shorter events, 0.7 us)
Async XLA Ops:
  0.6 17.9 %copy-start = (bf16[512,384]{1,0:T(8,128)(2,1)S(1)}, bf16[512,384]{1,0:T(8,128)(2,1)}, u32[]{:S(2)}) copy-start(bf16[512,384]{1,0:T(8,128)(2,1)} %param.4) | copy-start | bytes 1179652
  0.6 17.9 %copy-start.2 = (bf16[384,768]{1,0:T(8,128)(2,1)S(1)}, bf16[384,768]{1,0:T(8,128)(2,1)}, u32[]{:S(2)}) copy-start(bf16[384,768]{1,0:T(8,128)(2,1)} %param.6) | copy-start | bytes 1769476
  2.3 18.6 %copy-start.1 = (bf16[768,384]{1,0:T(8,128)(2,1)S(1)}, bf16[768,384]{1,0:T(8,128)(2,1)}, u32[]{:S(2)}) copy-start(bf16[768,384]{1,0:T(8,128)(2,1)} %param.7) | copy-start | bytes 1769476
  2.3 18.5 %copy-start.3 = (bf16[512,384]{1,0:T(8,128)(2,1)S(1)}, bf16[512,384]{1,0:T(8,128)(2,1)}, u32[]{:S(2)}) copy-start(bf16[512,384]{1,0:T(8,128)(2,1)} %param.5) | copy-start | bytes 1179652
  2.3 18.5 %collective-permute-start.1 = (f32[256,768]{1,0:T(8,128)S(1)}, f32[256,768]{1,0:T(8,128)}, u32[]{:S(2)}, u32[]{:S(2)}) collective-permute-start(f32[256,768]{1,0:T(8,128)S(1)} %fusion.17), channel_id=1, source_target_pairs={{0,32},{32,0},{1,33},{33,1},{2,34},{34,2},{3,35},{35,3},{4,36},{36... | collective-permute-start | bytes 2359304 | tf_op jit(solution)/shard_map/ppermute | solution.py:67
  18.9 4.3 %collective-permute-start = (f32[256,768]{1,0:T(8,128)S(1)}, f32[256,768]{1,0:T(8,128)}, u32[]{:S(2)}, u32[]{:S(2)}) collective-permute-start(f32[256,768]{1,0:T(8,128)S(1)} %fusion.20), channel_id=1, source_target_pairs={{0,32},{32,0},{1,33},{33,1},{2,34},{34,2},{3,35},{35,3},{4,36},{36... | collective-permute-start | bytes 2359304 | tf_op jit(solution)/shard_map/ppermute | solution.py:67
  40.4 20.3 %all-to-all-start.1 = ((f16[4,16,1536]{2,1,0:T(8,128)(2,1)}), f16[4,16,1536]{2,1,0:T(8,128)(2,1)S(1)}, u32[]{:S(2)}, u32[]{:S(2)}) async-start(f16[4,16,1536]{2,1,0:T(8,128)(2,1)} %bitcast.1), calls=%async_computation.1 | async-start | bytes 393216 | tf_op jit(solution)/shard_map/all_to_all | solution.py:62
  47.6 13.3 %collective-permute-start.2 = (bf16[768,384]{1,0:T(8,128)(2,1)S(1)}, bf16[768,384]{1,0:T(8,128)(2,1)S(1)}, u32[]{:S(2)}, u32[]{:S(2)}) collective-permute-start(bf16[768,384]{1,0:T(8,128)(2,1)S(1)} %copy-done.1), channel_id=1, source_target_pairs={{0,32},{32,0},{1,33},{33,1},{2,34},{34,2},{3,35},{35,3},{4,36},{36... | collective-permute-start | bytes 1769480 | tf_op jit(solution)/shard_map/ppermute | solution.py:67
  51.0 36.5 %collective-permute-start.3 = (bf16[384,768]{1,0:T(8,128)(2,1)S(1)}, bf16[384,768]{1,0:T(8,128)(2,1)S(1)}, u32[]{:S(2)}, u32[]{:S(2)}) collective-permute-start(bf16[384,768]{1,0:T(8,128)(2,1)S(1)} %copy-done.2), channel_id=1, source_target_pairs={{0,32},{32,0},{1,33},{33,1},{2,34},{34,2},{3,35},{35,3},{4,36},{36... | collective-permute-start | bytes 1769480 | tf_op jit(solution)/shard_map/ppermute | solution.py:67
  89.3 26.6 %all-to-all-start.2 = ((bf16[8,64,768]{2,1,0:T(8,128)(2,1)}), bf16[8,64,768]{2,1,0:T(8,128)(2,1)S(1)}, u32[]{:S(2)}, u32[]{:S(2)}) async-start(bf16[8,64,768]{2,1,0:T(8,128)(2,1)} %bitcast.4), calls=%async_computation.2 | async-start | bytes 1572864 | tf_op jit(solution)/shard_map/all_to_all | solution.py:62
  104.0 4.2 %collective-permute-start.4 = (bf16[256,1536]{1,0:T(8,128)(2,1)S(1)}, bf16[256,1536]{1,0:T(8,128)(2,1)S(1)}, u32[]{:S(2)}, u32[]{:S(2)}) collective-permute-start(bf16[256,1536]{1,0:T(8,128)(2,1)S(1)} %all_gather.7), channel_id=1, source_target_pairs={{0,32},{32,0},{1,33},{33,1},{2,34},{34,2},{3,35},{35,3},{4,36},{36... | collective-permute-start | bytes 2359304 | tf_op jit(solution)/shard_map/ppermute | solution.py:67
  116.8 18.3 %all-to-all-start.3 = ((f16[8,16,768]{2,1,0:T(8,128)(2,1)}), f16[8,16,768]{2,1,0:T(8,128)(2,1)S(1)}, u32[]{:S(2)}, u32[]{:S(2)}) async-start(f16[8,16,768]{2,1,0:T(8,128)(2,1)} %bitcast.8), calls=%async_computation.3 | async-start | bytes 393216 | tf_op jit(solution)/shard_map/all_to_all | solution.py:62
